TPU v7x, 32 devices: a whole 2x2x4 slice. The times are simulated.
32 devices in a mesh: dp: 8 (over z, core), seq: 4 (over y, x).
Axes of the slice: x: 2, y: 2, z: 4, core: 2. Of those that a mesh axis runs over, the one named last changes fastest.
Arguments:
- tokens: bfloat16 [4096, 1280], P(('dp', 'seq')), parts along dimension 0, may hold values from -6 to 6
- segment_ids: int32 [4096], P('dp'), parts along dimension 0, may hold values from 0 to 7, as said below
- w_qkv: bfloat16 [1280, 3840], P(None, 'seq')
- w_out: bfloat16 [1280, 1280], P('seq'), may hold values from -0.15625 to 0.15625
- w_merge: bfloat16 [5120, 4096], P(None, 'seq'), may hold values from -0.078125 to 0.078125
- gain_attn: float32 [1280], replicated, may hold values from 0.1 to 1.9
- gain_merge: float32 [1280], replicated, may hold values from 0.1 to 1.9
Outputs:
- merged_out: bfloat16 [1024, 4096], P(('dp', 'seq')), parts along dimension 0
There are 8 independent parts, one for each index of `dp`. A program takes and returns all parts, laid end to end along the dimension named above; an argument that names none is the same for every part. Nothing has to cross between parts.
Inputs may be any that keep to these rules, and one draw needn't show every extreme that they name: `segment_ids`: Non-decreasing along the packed tokens, starting at 0, rising by 0 or 1 from one token to the next, and equal within every aligned group of 4 tokens (an image's 2x2 patch blocks are stored together). There are exactly 8 images.
All inputs are finite; a program needn't handle non-finite values.
Results may differ from a plain program's by a relative error of at most 0.011.
Values may be sent and summed in bfloat16 or wider, within the bound.
A program may use at most 64 MiB of HBM per device.

v0:
```python
import jax
import jax.numpy as jnp
from jax import lax
from jax.sharding import PartitionSpec as P

D = 1280
HEADS = 16
HEAD_DIM = 80


def layer_norm(vector, scale_gain):
    average = jnp.mean(vector, axis=-1, keepdims=True)
    centred = vector - average
    spread_sq = jnp.mean(centred * centred, axis=-1, keepdims=True)
    return centred * lax.rsqrt(spread_sq + 1e-06) * scale_gain


def per_device(tokens, segment_ids, w_qkv, w_out, w_merge, gain_attn, gain_merge):
    group_size = lax.axis_size("seq")
    tok_local = tokens.shape[0]
    all_tokens = tok_local * group_size
    local_heads = HEADS // group_size
    residual = tokens.astype(jnp.float32)
    normed = layer_norm(residual, gain_attn).astype(jnp.bfloat16)
    qkv_rows = jnp.dot(
        lax.all_gather(normed, "seq", axis=0, tiled=True), w_qkv, preferred_element_type=jnp.float32
    ).astype(jnp.bfloat16)
    qkv = qkv_rows.reshape(all_tokens, local_heads, 3, HEAD_DIM)
    key_rows = qkv[:, :, 1, :]
    value_rows = qkv[:, :, 2, :]
    block_rows = min(512, all_tokens)
    block_count = all_tokens // block_rows
    scale_factor = HEAD_DIM ** (-0.5)

    def masked_scores(queries, query_ids, key_part, key_ids):
        scores = (
            jnp.einsum("qhd,khd->hqk", queries, key_part, preferred_element_type=jnp.float32)
            * scale_factor
        )
        same_image = (query_ids[:, None] == key_ids[None, :])[None, :, :]
        return (jnp.where(same_image, scores, -jnp.inf), same_image)

    def query_block(block_index):
        query_start = block_index * block_rows
        queries = lax.dynamic_slice_in_dim(qkv, query_start, block_rows, 0)[:, :, 0, :]
        query_ids = lax.dynamic_slice_in_dim(segment_ids, query_start, block_rows, 0)
        scores, same_image = masked_scores(queries, query_ids, key_rows, segment_ids)
        row_max = jnp.max(scores, axis=-1, keepdims=True)
        expo = jnp.where(same_image, jnp.exp(scores - row_max), 0.0)
        row_sum = jnp.sum(expo, axis=-1)
        probs = expo.astype(jnp.bfloat16)
        summed = jnp.einsum("hqk,khd->qhd", probs, value_rows, preferred_element_type=jnp.float32)
        result = summed / row_sum.T[:, :, None]
        return result.astype(jnp.bfloat16).reshape(block_rows, local_heads * HEAD_DIM)

    attended = lax.map(query_block, jnp.arange(block_count, dtype=jnp.int32)).reshape(
        all_tokens, local_heads * HEAD_DIM
    )
    back = lax.all_to_all(attended, "seq", split_axis=0, concat_axis=1, tiled=True)
    projected_attn = jnp.dot(
        back, lax.all_gather(w_out, "seq", axis=0, tiled=True), preferred_element_type=jnp.float32
    )
    hidden = residual + projected_attn
    normed_two = layer_norm(hidden, gain_merge).astype(jnp.bfloat16)
    merged = normed_two.reshape(tok_local // 4, 4 * D)
    column_block = jnp.dot(
        lax.all_gather(merged, "seq", axis=0, tiled=True),
        w_merge,
        preferred_element_type=jnp.float32,
    ).astype(jnp.bfloat16)
    return lax.all_to_all(column_block, "seq", split_axis=0, concat_axis=1, tiled=True)


def solution(mesh):
    placed = (
        P(("dp", "seq"), None),
        P("dp"),
        P(None, "seq"),
        P("seq", None),
        P(None, "seq"),
        P(),
        P(),
    )
    return jax.shard_map(
        per_device, mesh=mesh, in_specs=placed, out_specs=P(("dp", "seq"), None), check_vma=False
    )
```

profile of v0, /device:TPU:0, one launch (start us, length us, event | category | flops | bytes accessed | tf_op | source)
XLA Modules:
  0.0 147.7 jit_solution(10997968282334714825)
XLA Ops:
  6.5 0.0 copy-start
  6.5 0.0 all-gather.4.cloned.1.call-start
  6.5 1.2 convert_reduce_fusion
  7.8 1.2 fusion.18
  9.0 1.9 %fusion.20 = bf16[128,1280]{1,0:T(8,128)(2,1)} fusion(bf16[128,1280]{1,0:T(8,128)(2,1)} %param.7, f32[1280]{0:T(1024)} %param.12, f32[128]{0:T(128)S(1)} %add_rsqrt_fusion.1, f32[128]{0:T(128)S(1)} %broadcast_multiply_fusion.1), kind=kLoop, calls=%fused_computation.21 | loop fusion | flops 819200 | bytes 661504 | tf_op jit(solution)/shard_map/convert_element_type | solution.py:24
  11.0 0.0 all-gather.4.cloned.1.call-update
  11.0 0.0 all-gather.6.cloned.1.call-start
  11.0 0.7 all-gather.6.cloned.1.call-update
  11.7 0.0 all-gather.8.cloned.1.call-start
  11.8 1.0 broadcast_compare_fusion
  12.8 29.9 %all-gather.4.cloned.1.call-done = bf16[512,1280]{1,0:T(8,128)(2,1)} async-done(((bf16[128,1280]{1,0:T(8,128)(2,1)}), bf16[512,1280]{1,0:T(8,128)(2,1)}) %all-gather.4.cloned.1.call-update) | async-done | bytes 1310736 | tf_op jit(solution)/shard_map/all_gather | solution.py:26
  42.6 0.0 copy-done
  42.6 3.8 %convolution_convert_fusion = bf16[512,960]{0,1:T(8,128)(2,1)} fusion(bf16[512,1280]{1,0:T(8,128)(2,1)} %all-gather.4.cloned.1.call-done, bf16[1280,960]{0,1:T(8,128)(2,1)S(1)} %copy-done), kind=kOutput, calls=%fused_computation.10 | convolution fusion | flops 1258782720 | bytes 4751360 | tf_op jit(solution)/shard_map/dot_general | solution.py:25
  46.4 4.5 %fusion.26 = (f32[4,512]{1,0:T(4,128)S(1)}, bf16[4,512,512]{1,2,0:T(8,128)(2,1)}) fusion(pred[512,512]{0,1:T(8,128)(4,1)S(1)} %broadcast_compare_fusion, bf16[512,4,3,80]{0,3,2,1:T(8,128)(2,1)} %bitcast.58), kind=kOutput, calls=%fused_computation.36 | convolution fusion | flops 174064128 | bytes 3284992 | tf_op jit(solution)/shard_map/while/body/eval_jaxpr/sub | solution.py:49
  50.9 0.0 copy-start.1
  50.9 2.5 %fusion.13 = bf16[512,4,80]{0,2,1:T(8,128)(2,1)S(1)} fusion(bf16[4,512,512]{1,2,0:T(8,128)(2,1)} %get-tuple-element.16, bf16[512,4,3,80]{0,3,2,1:T(8,128)(2,1)} %bitcast.59, f32[512,4]{0,1:T(4,128)S(1)} %bitcast.60), kind=kOutput, calls=%fused_computation.13 | convolution fusion | flops 168099840 | bytes 2760704 | tf_op jit(solution)/shard_map/while/body/eval_jaxpr/hqk,khd->qhd/dot_general | solution.py:52
  53.4 0.1 all_to_all.28
  53.5 0.0 copy-start.2
  53.5 13.2 %all_to_all.38 = bf16[4,128,320]{1,2,0:T(8,128)(2,1)S(1)} all-to-all(bf16[4,128,320]{1,2,0:T(8,128)(2,1)S(1)} %copy.17), channel_id=1, replica_groups=mesh['dp'=8,'seq'=4] {'seq'}, dimensions={0} | all-to-all | bytes 655360 | tf_op jit(solution)/shard_map/all_to_all | solution.py:59
  66.8 26.3 %all-gather.6.cloned.1.call-done = bf16[1280,1280]{1,0:T(8,128)(2,1)} async-done(((bf16[320,1280]{1,0:T(8,128)(2,1)}), bf16[1280,1280]{1,0:T(8,128)(2,1)}) %all-gather.6.cloned.1.call-update) | async-done | bytes 3276816 | tf_op jit(solution)/shard_map/all_gather | solution.py:61
  93.1 0.0 copy-done.1
  93.1 2.7 %fusion.27 = (f32[128]{0:T(128)S(1)}, f32[128,1280]{1,0:T(8,128)S(1)}) fusion(bf16[128,1280]{0,1:T(8,128)(2,1)S(1)} %bitcast.55, bf16[1280,1280]{1,0:T(8,128)(2,1)} %all-gather.6.cloned.1.call-done, bf16[128,1280]{1,0:T(8,128)(2,1)S(1)} %copy-done.1), kind=kOutput, calls=%fused_computation.37 | convolution fusion | flops 419921792 | bytes 4588032 | tf_op jit(solution)/shard_map/dot_general | solution.py:60
  95.8 0.2 multiply_reduce_fusion
  96.0 0.0 copy-done.2
  96.0 0.2 multiply_convert_fusion
  96.2 1.0 reshape.74
  97.1 0.0 all-gather.8.cloned.1.call-update
  97.2 29.0 %all-gather.8.cloned.1.call-done = bf16[128,5120]{1,0:T(8,128)(2,1)} async-done(((bf16[32,5120]{1,0:T(8,128)(2,1)}), bf16[128,5120]{1,0:T(8,128)(2,1)}) %all-gather.8.cloned.1.call-update) | async-done | bytes 1310736 | tf_op jit(solution)/shard_map/all_gather | solution.py:67
  126.1 5.9 %convolution_convert_fusion.1 = bf16[128,1024]{1,0:T(8,128)(2,1)S(1)} fusion(bf16[128,5120]{1,0:T(8,128)(2,1)} %all-gather.8.cloned.1.call-done, bf16[5120,1024]{1,0:T(8,128)(2,1)} %param.11), kind=kOutput, calls=%fused_computation.14 | convolution fusion | flops 1342308352 | bytes 12058624 | tf_op jit(solution)/shard_map/dot_general | solution.py:66
  132.0 8.4 %all_to_all.39 = bf16[4,32,1024]{2,1,0:T(8,128)(2,1)S(1)} all-to-all(bf16[4,32,1024]{2,1,0:T(8,128)(2,1)S(1)} %bitcast.56), channel_id=1, replica_groups=mesh['dp'=8,'seq'=4] {'seq'}, dimensions={0} | all-to-all | bytes 524288 | tf_op jit(solution)/shard_map/all_to_all | solution.py:71
  140.4 0.7 copy.23
  (5 shorter events, 0.1 us)
Async XLA Ops:
  6.5 36.1 %copy-start = (bf16[1280,960]{0,1:T(8,128)(2,1)S(1)}, bf16[1280,960]{0,1:T(8,128)(2,1)}, u32[]{:S(2)}) copy-start(bf16[1280,960]{0,1:T(8,128)(2,1)} %param.9) | copy-start | bytes 7372804
  6.5 36.1 %all-gather.4.cloned.1.call-start = ((), (), s32[]{:S(2)}) async-start(), calls=%async_computation.2 | async-start | bytes 1638400 | tf_op jit(solution)/shard_map/all_gather | solution.py:26
  11.0 82.1 %all-gather.6.cloned.1.call-start = ((), (), s32[]{:S(2)}) async-start(), calls=%async_computation.3 | async-start | bytes 4096000 | tf_op jit(solution)/shard_map/all_gather | solution.py:61
  11.7 114.4 %all-gather.8.cloned.1.call-start = ((), (), s32[]{:S(2)}) async-start(), calls=%async_computation.4 | async-start | bytes 1638400 | tf_op jit(solution)/shard_map/all_gather | solution.py:67
  50.9 42.2 %copy-start.1 = (bf16[128,1280]{1,0:T(8,128)(2,1)S(1)}, bf16[128,1280]{1,0:T(8,128)(2,1)}, u32[]{:S(2)}) copy-start(bf16[128,1280]{1,0:T(8,128)(2,1)} %param.7) | copy-start | bytes 983044
  53.5 42.5 %copy-start.2 = (f32[1280]{0:T(1024)S(1)}, f32[1280]{0:T(1024)}, u32[]{:S(2)}) copy-start(f32[1280]{0:T(1024)} %param.13) | copy-start | bytes 15364
Sparse Core Ops, SparseCore 0:
  11.1 31.4 all-gather.3
  44.5 48.5 all-gather.5
  97.3 28.7 all-gather.7
where the time goes:
time: 148 us
  waiting for transfers between devices  85.9 us (58%)
  blocking collectives  21.6 us (15%)
  matrix products  19.3 us (13%)
  between operations  13.2 us (9%)
  other arithmetic  5.77 us (4%)
  local copies, waits for them, and re-layouts  1.82 us (1%)
    all_gather x1, waiting for transfers between devices, per_device(): lax.all_gather(normed, 'seq', axis=0, tiled=True)  29.9 us
    all_gather x1, waiting for transfers between devices, per_device(): lax.all_gather(merged, 'seq', axis=0, tiled=True)  29 us
    all_gather x1, waiting for transfers between devices, per_device(): lax.all_gather(w_out, 'seq', axis=0, tiled=True)  26.3 us
    all_to_all x1, blocking collectives, per_device(): lax.all_to_all(attended, 'seq', split_axis=0, concat_axis=1, tiled=True)  13.2 us
    all_to_all x1, blocking collectives, per_device(): lax.all_to_all(column_block, 'seq', split_axis=0, concat_axis=1, tiled=True)  8.38 us
    dot_general x1, matrix products, per_device(): jnp.dot(lax.all_gather(merged, 'seq', axis=0, tiled=True), w_merge, prefe...  5.91 us
    sub x1, matrix products, query_block(): expo = jnp.where(same_image, jnp.exp(scores - row_max), 0.0)  4.5 us
    dot_general x1, matrix products, per_device(): jnp.dot(lax.all_gather(normed, 'seq', axis=0, tiled=True), w_qkv, preferr...  3.76 us
  transfers between devices with their start and end apart: 3, of which 3 were waited for; matrix products, arithmetic and copies ran while one was open for 8% of the time, Pallas kernels for 0%

commit v1 on v0

v1 whole, which is shorter than its diff:
```python
import functools

import jax
import jax.numpy as jnp
from jax import lax
from jax.experimental import pallas as pl
from jax.experimental.pallas import tpu as pltpu
from jax.sharding import PartitionSpec as P

HEADS = 16
HEAD_DIM = 80
LOG2E = 1.4426950408889634
MESH = pl.DeviceIdType.MESH


def layer_norm(vector, scale_gain):
    average = jnp.mean(vector, axis=-1, keepdims=True)
    centred = vector - average
    spread_sq = jnp.mean(centred * centred, axis=-1, keepdims=True)
    return centred * lax.rsqrt(spread_sq + 1e-06) * scale_gain


def block_kernel(
    n, tok_ref, ids_ref, wqkv_hbm, wout_hbm, wmerge_hbm, ga_ref, gm_ref, out_ref,
    wqkv, wout, wmerge, nslots, qs, ks, vs, kid, att, psend, pslots, own, flat, mslots, obuf,
    local_sem, a_send, a_recv, p_send, p_recv, m_send, m_recv, o_send, o_recv,
):
    me = lax.axis_index("seq")
    dp = lax.axis_index("dp")
    rows = tok_ref.shape[0]
    width = tok_ref.shape[1]
    heads = qs.shape[0]
    bits = n.bit_length() - 1
    quarter = rows // 4
    cols = wmerge_hbm.shape[1]

    def peer(d):
        total = 0
        for b in range(bits):
            total = total + (((me // (1 << b)) + (d // (1 << b))) % 2) * (1 << b)
        return total

    def remote(src, dst, send, recv, d):
        return pltpu.make_async_remote_copy(
            src_ref=src, dst_ref=dst, send_sem=send, recv_sem=recv,
            device_id=(dp, peer(d)), device_id_type=MESH,
        )

    def copy_a(d):
        return remote(nslots.at[0], nslots.at[d], a_send.at[d], a_recv.at[d], d)

    def copy_p(d):
        return remote(psend.at[d], pslots.at[d], p_send.at[d], p_recv.at[d], d)

    def copy_m(j, d):
        return remote(
            mslots.at[j, pl.ds(0, quarter)],
            mslots.at[j, pl.ds(d * quarter, quarter)],
            m_send.at[j, d], m_recv.at[j, d], d,
        )

    def copy_o(d):
        return remote(
            obuf.at[pl.ds(d * quarter, quarter)],
            out_ref.at[:, pl.ds(pl.multiple_of(me * cols, 128), cols)],
            o_send.at[d], o_recv.at[d], d,
        )

    barrier = pltpu.get_barrier_semaphore()
    for d in range(1, n):
        pl.semaphore_signal(barrier, inc=1, device_id=(dp, peer(d)), device_id_type=MESH)
    load_qkv = pltpu.make_async_copy(wqkv_hbm, wqkv, local_sem.at[0])
    load_out = pltpu.make_async_copy(wout_hbm, wout, local_sem.at[1])
    load_merge = pltpu.make_async_copy(wmerge_hbm, wmerge, local_sem.at[2])
    load_qkv.start()
    load_out.start()
    load_merge.start()

    nslots[0] = layer_norm(tok_ref[...].astype(jnp.float32), ga_ref[...]).astype(jnp.bfloat16)
    pl.semaphore_wait(barrier, n - 1)
    for d in range(n - 1, 0, -1):
        copy_a(d).start()

    for d in range(n):
        kid[0:1, d * rows:(d + 1) * rows] = ids_ref[pl.ds(peer(d), 1), :].astype(jnp.float32)

    load_qkv.wait()
    load_out.wait()

    def qkv_step(d, carry):
        @pl.when(d > 0)
        def _():
            copy_a(d).wait_recv()

        prod = jnp.dot(nslots[d], wqkv[...], preferred_element_type=jnp.float32)
        prod = prod.astype(jnp.bfloat16)
        at = pl.ds(pl.multiple_of(d * rows, rows), rows)
        for h in range(heads):
            base = 3 * HEAD_DIM * h
            qs[h, at, :] = prod[:, base:base + HEAD_DIM]
            ks[h, at, :] = prod[:, base + HEAD_DIM:base + 2 * HEAD_DIM]
            vs[h, at, :] = prod[:, base + 2 * HEAD_DIM:base + 3 * HEAD_DIM]
        return carry

    lax.fori_loop(0, n, qkv_step, 0)

    factor = HEAD_DIM ** (-0.5) * LOG2E

    def attend_step(i, carry):
        d = n - 1 - i
        id_row = ids_ref[pl.ds(peer(d), 1), :].astype(jnp.float32)
        query_ids = jnp.broadcast_to(id_row, (rows, rows)).T[:, 0:1]
        same_image = query_ids == kid[...]
        at = pl.ds(pl.multiple_of(d * rows, rows), rows)
        for h in range(heads):
            scores = lax.dot_general(
                qs[h, at, :], ks[h], (((1,), (1,)), ((), ())),
                preferred_element_type=jnp.float32,
            )
            scores = jnp.where(same_image, scores * factor, -jnp.inf)
            expo = jnp.exp2(scores - jnp.max(scores, axis=-1, keepdims=True))
            row_sum = jnp.sum(expo, axis=-1, keepdims=True)
            summed = jnp.dot(
                expo.astype(jnp.bfloat16), vs[h], preferred_element_type=jnp.float32
            )
            att[:, h * HEAD_DIM:(h + 1) * HEAD_DIM] = (summed / row_sum).astype(jnp.bfloat16)
        part = jnp.dot(att[...], wout[...], preferred_element_type=jnp.float32)

        @pl.when(d > 0)
        def _():
            psend[d] = part.astype(jnp.bfloat16)
            copy_p(d).start()

        @pl.when(d == 0)
        def _():
            own[...] = part

        return carry

    lax.fori_loop(0, n, attend_step, 0)

    hidden = own[...] + tok_ref[...].astype(jnp.float32)
    for d in range(n - 1, 0, -1):
        copy_p(d).wait_recv()
        hidden = hidden + pslots[d].astype(jnp.float32)
    normed_two = layer_norm(hidden, gm_ref[...])
    lanes = flat.shape[2]
    for c in range(width // lanes):
        flat[c] = normed_two[:, c * lanes:(c + 1) * lanes]
    for j in range(4):
        for c in range(width // lanes):
            mslots[j, 0:quarter, c * lanes:(c + 1) * lanes] = flat[
                c, pl.ds(j, quarter, stride=4), :
            ].astype(jnp.bfloat16)
        for d in range(n - 1, 0, -1):
            copy_m(j, d).start()

    load_merge.wait()
    acc = None
    for j in range(4):
        for d in range(1, n):
            copy_m(j, d).wait_recv()
        part = jnp.dot(
            mslots[j], wmerge[j * width:(j + 1) * width, :], preferred_element_type=jnp.float32
        )
        acc = part if acc is None else acc + part
    obuf[...] = acc.astype(jnp.bfloat16)
    for d in range(n - 1, 0, -1):
        copy_o(d).start()
    out_ref[:, pl.ds(pl.multiple_of(me * cols, 128), cols)] = obuf[0:quarter, :]

    for d in range(1, n):
        copy_a(d).wait_send()
        copy_p(d).wait_send()
        for j in range(4):
            copy_m(j, d).wait_send()
    for d in range(1, n):
        copy_o(d).wait_send()
        copy_o(d).wait_recv()


def per_device(tokens, segment_ids, w_qkv, w_out, w_merge, gain_attn, gain_merge):
    n = lax.axis_size("seq")
    rows, width = tokens.shape
    heads = HEADS // n
    quarter = rows // 4
    cols = w_merge.shape[1]
    total = n * rows
    vmem = pl.BlockSpec(memory_space=pltpu.VMEM)
    hbm = pl.BlockSpec(memory_space=pl.ANY)
    bf16 = jnp.bfloat16
    dma = pltpu.SemaphoreType.DMA
    return pl.pallas_call(
        functools.partial(block_kernel, n),
        out_shape=jax.ShapeDtypeStruct((quarter, n * cols), bf16),
        in_specs=[vmem, vmem, hbm, hbm, hbm, vmem, vmem],
        out_specs=vmem,
        scratch_shapes=[
            pltpu.VMEM(w_qkv.shape, bf16),
            pltpu.VMEM(w_out.shape, bf16),
            pltpu.VMEM(w_merge.shape, bf16),
            pltpu.VMEM((n, rows, width), bf16),
            pltpu.VMEM((heads, total, HEAD_DIM), bf16),
            pltpu.VMEM((heads, total, HEAD_DIM), bf16),
            pltpu.VMEM((heads, total, HEAD_DIM), bf16),
            pltpu.VMEM((1, total), jnp.float32),
            pltpu.VMEM((rows, heads * HEAD_DIM), bf16),
            pltpu.VMEM((n, rows, width), bf16),
            pltpu.VMEM((n, rows, width), bf16),
            pltpu.VMEM((rows, width), jnp.float32),
            pltpu.VMEM((width // 128, rows, 128), jnp.float32),
            pltpu.VMEM((4, n * quarter, width), bf16),
            pltpu.VMEM((n * quarter, cols), bf16),
            dma((3,)),
            dma((n,)),
            dma((n,)),
            dma((n,)),
            dma((n,)),
            dma((4, n)),
            dma((4, n)),
            dma((n,)),
            dma((n,)),
        ],
        compiler_params=pltpu.CompilerParams(
            collective_id=0, has_side_effects=True, vmem_limit_bytes=56 * 1024 * 1024
        ),
    )(
        tokens, segment_ids.reshape(n, rows), w_qkv, w_out, w_merge,
        gain_attn.reshape(1, width), gain_merge.reshape(1, width),
    )


def solution(mesh):
    placed = (
        P(("dp", "seq"), None),
        P("dp"),
        P(None, "seq"),
        P("seq", None),
        P(None, "seq"),
        P(),
        P(),
    )
    return jax.shard_map(
        per_device, mesh=mesh, in_specs=placed, out_specs=P(("dp", "seq"), None), check_vma=False
    )
```

time: 148 us -> 71 us (0.48)
  waiting for transfers between devices: 85.9 us -> 0 us
  Pallas kernels: 0 us -> 61.9 us
  blocking collectives: 21.6 us -> 0 us
  matrix products: 19.3 us -> 0 us
  between operations: 13.2 us -> 0.01 us
  local copies, waits for them, and re-layouts: 1.82 us -> 8.76 us
  other arithmetic: 5.77 us -> 0 us
    all_gather x3 -> x0, waiting for transfers between devices: 85.2 us -> none  [the longest x1 29.9 us: per_device(): lax.all_gather(normed, 'seq', axis=0, tiled=True)]
    pallas_call x0 -> x1, Pallas kernels: none -> 61.9 us  [per_device(): pl.pallas_call(functools.partial(block_kernel, n), out_shape=jax.ShapeDty...]
    all_to_all x2 -> x0, blocking collectives: 21.6 us -> none  [the longest x1 13.2 us: per_device(): lax.all_to_all(attended, 'seq', split_axis=0, concat_axis=1, tiled=True)]
    dot_general x4 -> x0, matrix products: 14.8 us -> none  [the longest x1 5.91 us: per_device(): jnp.dot(lax.all_gather(merged, 'seq', axis=0, tiled=True), w_merge, prefe...]
    unnamed x6 -> x2, local copies, waits for them, and re-layouts: 0.01 us -> 6.18 us
    sub x1 -> x0, matrix products: 4.5 us -> none  [query_block(): expo = jnp.where(same_image, jnp.exp(scores - row_max), 0.0)]
    reduce_sum x3 -> x0, other arithmetic: 2.67 us -> none  [the longest x2 1.43 us: layer_norm(): spread_sq = jnp.mean(centred * centred, axis=-1, keepdims=True)]
    convert_element_type x2 -> x0, other arithmetic: 2.1 us -> none  [the longest x1 1.94 us: per_device(): normed = layer_norm(residual, gain_attn).astype(jnp.bfloat16)]
  transfers between devices with their start and end apart: 3 -> 0, of which waited for: 3 -> 0; matrix products, arithmetic and copies ran while one was open for 8% -> 0% of each run, Pallas kernels for 0% -> 0%
where the time goes in v1:
time: 71 us; the launch traced here: 70.7 us
  Pallas kernels  61.9 us (87%)
  local copies, waits for them, and re-layouts  8.76 us (12%)
    pallas_call x1, Pallas kernels, per_device(): pl.pallas_call(functools.partial(block_kernel, n), out_shape=jax.ShapeDty...  61.9 us
    unnamed x2, local copies, waits for them, and re-layouts  6.18 us

profile of v1, /device:TPU:0, one launch (start us, length us, event | category | flops | bytes accessed | tf_op | source)
XLA Modules:
  0.0 70.7 jit_solution(16245280590037861903)
XLA Ops:
  0.0 1.3 %reshape.10.ga_ref = f32[1,1280]{1,0:T(1,128)} reshape(f32[1280]{0:T(1024)} %param.12) | data formatting | bytes 10240 | tf_op jit(solution)/shard_map/reshape | solution.py:229
  1.3 1.3 %reshape.11.gm_ref = f32[1,1280]{1,0:T(1,128)} reshape(f32[1280]{0:T(1024)} %param.13) | data formatting | bytes 10240 | tf_op jit(solution)/shard_map/reshape | solution.py:229
  2.6 4.5 %copy.8.wqkv_hbm = bf16[1280,960]{1,0:T(8,128)(2,1)} copy(bf16[1280,960]{0,1:T(8,128)(2,1)} %param.9) | data formatting | bytes 4915200 | tf_op args[2]
  7.1 61.9 %shard_map.73 = bf16[32,4096]{1,0:T(8,128)(2,1)} custom-call(bf16[128,1280]{1,0:T(8,128)(2,1)} %tok_ref.1, s32[4,128]{1,0:T(4,128)} %bitcast.1, bf16[1280,960]{1,0:T(8,128)(2,1)} %copy.8.wqkv_hbm, bf16[320,1280]{1,0:T(8,128)(2,1)} %wout_hbm.1, bf16[5120,1024]{1,0:T(8,128)(2,1)} %wmerge_hbm.1, f32[1,1280]{1,0:T(1,128)} %reshape.10.ga_ref, ...), custom_call_target="tpu_custom_call" | custom-call | tf_op jit(solution)/shard_map/pallas_call | solution.py:193
  69.0 1.7 %copy.10 = bf16[32,4096]{1,0:T(8,128)(2,1)} copy(bf16[32,4096]{1,0:T(8,128)(2,1)} %shard_map.73) | data formatting | bytes 524288

commit v2 on v1

--- a/solution.py
+++ b/solution.py
@@ -22,7 +22,7 @@
 
 def block_kernel(
     n, tok_ref, ids_ref, wqkv_hbm, wout_hbm, wmerge_hbm, ga_ref, gm_ref, out_ref,
-    wqkv, wout, wmerge, nslots, qs, ks, vs, kid, att, psend, pslots, own, flat, mslots, obuf,
+    wqkv, wout, wmerge, nslots, qs, ks, vs, key_ids, bias, att, psend, pslots, own, flat, mslots, obuf,
     local_sem, a_send, a_recv, p_send, p_recv, m_send, m_recv, o_send, o_recv,
 ):
     me = lax.axis_index("seq")
@@ -47,7 +47,9 @@
         )
 
     def copy_a(d):
-        return remote(nslots.at[0], nslots.at[d], a_send.at[d], a_recv.at[d], d)
+        return remote(
+            nslots.at[pl.ds(0, rows)], nslots.at[pl.ds(d * rows, rows)], a_send.at[d], a_recv.at[d], d,
+        )
 
     def copy_p(d):
         return remote(psend.at[d], pslots.at[d], p_send.at[d], p_recv.at[d], d)
@@ -76,74 +78,86 @@
     load_out.start()
     load_merge.start()
 
-    nslots[0] = layer_norm(tok_ref[...].astype(jnp.float32), ga_ref[...]).astype(jnp.bfloat16)
+    nslots[0:rows, :] = layer_norm(tok_ref[...].astype(jnp.float32), ga_ref[...].reshape(1, width)).astype(jnp.bfloat16)
     pl.semaphore_wait(barrier, n - 1)
     for d in range(n - 1, 0, -1):
         copy_a(d).start()
 
     for d in range(n):
-        kid[0:1, d * rows:(d + 1) * rows] = ids_ref[pl.ds(peer(d), 1), :].astype(jnp.float32)
+        id_row = ids_ref[pl.ds(peer(d), 1), :].astype(jnp.float32)
+        key_ids[d * rows:(d + 1) * rows, :] = jnp.broadcast_to(id_row, (rows, rows)).T
 
     load_qkv.wait()
     load_out.wait()
 
-    def qkv_step(d, carry):
-        @pl.when(d > 0)
-        def _():
-            copy_a(d).wait_recv()
-
-        prod = jnp.dot(nslots[d], wqkv[...], preferred_element_type=jnp.float32)
-        prod = prod.astype(jnp.bfloat16)
-        at = pl.ds(pl.multiple_of(d * rows, rows), rows)
+    def qkv_step(i, carry):
+        for side in range(2):
+            d = 2 * i + side
+
+            @pl.when(d > 0)
+            def _():
+                copy_a(d).wait_recv()
+
+        at = pl.ds(pl.multiple_of(i * 2 * rows, 2 * rows), 2 * rows)
         for h in range(heads):
-            base = 3 * HEAD_DIM * h
-            qs[h, at, :] = prod[:, base:base + HEAD_DIM]
-            ks[h, at, :] = prod[:, base + HEAD_DIM:base + 2 * HEAD_DIM]
-            vs[h, at, :] = prod[:, base + 2 * HEAD_DIM:base + 3 * HEAD_DIM]
+            for which in range(3):
+                base = HEAD_DIM * (3 * h + which)
+                prod = lax.dot_general(
+                    wqkv[base:base + HEAD_DIM, :], nslots[at, :], (((1,), (1,)), ((), ())),
+                    preferred_element_type=jnp.float32,
+                )
+                if which == 0:
+                    qs[h, :, at] = prod.astype(jnp.bfloat16)
+                elif which == 1:
+                    ks[h, at, :] = prod.T.astype(jnp.bfloat16)
+                else:
+                    vs[h, :, at] = prod.astype(jnp.bfloat16)
         return carry
 
-    lax.fori_loop(0, n, qkv_step, 0)
+    lax.fori_loop(0, n // 2, qkv_step, 0)
 
     factor = HEAD_DIM ** (-0.5) * LOG2E
 
     def attend_step(i, carry):
-        d = n - 1 - i
-        id_row = ids_ref[pl.ds(peer(d), 1), :].astype(jnp.float32)
-        query_ids = jnp.broadcast_to(id_row, (rows, rows)).T[:, 0:1]
-        same_image = query_ids == kid[...]
-        at = pl.ds(pl.multiple_of(d * rows, rows), rows)
+        first = n - 2 - 2 * i
+        at = pl.ds(pl.multiple_of(first * rows, 2 * rows), 2 * rows)
+        for side in range(2):
+            id_row = ids_ref[pl.ds(peer(first + side), 1), :].astype(jnp.float32)
+            bias[:, side * rows:(side + 1) * rows] = jnp.where(
+                key_ids[...] == id_row, 0.0, -jnp.inf
+            )
         for h in range(heads):
-            scores = lax.dot_general(
-                qs[h, at, :], ks[h], (((1,), (1,)), ((), ())),
-                preferred_element_type=jnp.float32,
-            )
-            scores = jnp.where(same_image, scores * factor, -jnp.inf)
-            expo = jnp.exp2(scores - jnp.max(scores, axis=-1, keepdims=True))
-            row_sum = jnp.sum(expo, axis=-1, keepdims=True)
-            summed = jnp.dot(
-                expo.astype(jnp.bfloat16), vs[h], preferred_element_type=jnp.float32
-            )
-            att[:, h * HEAD_DIM:(h + 1) * HEAD_DIM] = (summed / row_sum).astype(jnp.bfloat16)
-        part = jnp.dot(att[...], wout[...], preferred_element_type=jnp.float32)
-
-        @pl.when(d > 0)
-        def _():
-            psend[d] = part.astype(jnp.bfloat16)
-            copy_p(d).start()
-
-        @pl.when(d == 0)
-        def _():
-            own[...] = part
+            scores = jnp.dot(ks[h], qs[h, :, at], preferred_element_type=jnp.float32)
+            scores = scores * factor + bias[...]
+            expo = jnp.exp2(scores - jnp.max(scores, axis=0, keepdims=True))
+            row_sum = jnp.sum(expo, axis=0, keepdims=True)
+            summed = jnp.dot(vs[h], expo.astype(jnp.bfloat16), preferred_element_type=jnp.float32)
+            att[h * HEAD_DIM:(h + 1) * HEAD_DIM, :] = summed / row_sum
+        part = jnp.dot(
+            att[...].T.astype(jnp.bfloat16), wout[...], preferred_element_type=jnp.float32
+        )
+        for side in range(1, -1, -1):
+            d = first + side
+            half = part[side * rows:(side + 1) * rows, :]
+
+            @pl.when(d > 0)
+            def _():
+                psend[d] = half.astype(jnp.bfloat16)
+                copy_p(d).start()
+
+            @pl.when(d == 0)
+            def _():
+                own[...] = half
 
         return carry
 
-    lax.fori_loop(0, n, attend_step, 0)
+    lax.fori_loop(0, n // 2, attend_step, 0)
 
     hidden = own[...] + tok_ref[...].astype(jnp.float32)
     for d in range(n - 1, 0, -1):
         copy_p(d).wait_recv()
         hidden = hidden + pslots[d].astype(jnp.float32)
-    normed_two = layer_norm(hidden, gm_ref[...])
+    normed_two = layer_norm(hidden, gm_ref[...].reshape(1, width))
     lanes = flat.shape[2]
     for c in range(width // lanes):
         flat[c] = normed_two[:, c * lanes:(c + 1) * lanes]
@@ -196,15 +210,16 @@
         in_specs=[vmem, vmem, hbm, hbm, hbm, vmem, vmem],
         out_specs=vmem,
         scratch_shapes=[
-            pltpu.VMEM(w_qkv.shape, bf16),
+            pltpu.VMEM(w_qkv.shape[::-1], bf16),
             pltpu.VMEM(w_out.shape, bf16),
             pltpu.VMEM(w_merge.shape, bf16),
-            pltpu.VMEM((n, rows, width), bf16),
+            pltpu.VMEM((total, width), bf16),
+            pltpu.VMEM((heads, HEAD_DIM, total), bf16),
             pltpu.VMEM((heads, total, HEAD_DIM), bf16),
-            pltpu.VMEM((heads, total, HEAD_DIM), bf16),
-            pltpu.VMEM((heads, total, HEAD_DIM), bf16),
-            pltpu.VMEM((1, total), jnp.float32),
-            pltpu.VMEM((rows, heads * HEAD_DIM), bf16),
+            pltpu.VMEM((heads, HEAD_DIM, total), bf16),
+            pltpu.VMEM((total, rows), jnp.float32),
+            pltpu.VMEM((total, 2 * rows), jnp.float32),
+            pltpu.VMEM((heads * HEAD_DIM, 2 * rows), jnp.float32),
             pltpu.VMEM((n, rows, width), bf16),
             pltpu.VMEM((n, rows, width), bf16),
             pltpu.VMEM((rows, width), jnp.float32),
@@ -225,8 +240,7 @@
             collective_id=0, has_side_effects=True, vmem_limit_bytes=56 * 1024 * 1024
         ),
     )(
-        tokens, segment_ids.reshape(n, rows), w_qkv, w_out, w_merge,
-        gain_attn.reshape(1, width), gain_merge.reshape(1, width),
+        tokens, segment_ids.reshape(n, rows), w_qkv.T, w_out, w_merge, gain_attn, gain_merge,
     )
 
 

time: 71 us -> 66.1 us (0.931)
  local copies, waits for them, and re-layouts: 8.76 us -> 1.67 us
  Pallas kernels: 61.9 us -> 64.2 us
    unnamed x2 -> x1, local copies, waits for them, and re-layouts: 6.18 us -> 1.67 us
    reshape x2 -> x0, local copies, waits for them, and re-layouts: 2.58 us -> none  [the longest x1 1.29 us: per_device(): gain_attn.reshape(1, width)]
    pallas_call x1, Pallas kernels: 61.9 us -> 64.2 us  [per_device(): pl.pallas_call(functools.partial(block_kernel, n), out_shape=jax.ShapeDty...]
where the time goes in v2:
time: 66.1 us; the launch traced here: 65.9 us
  Pallas kernels  64.2 us (97%)
  local copies, waits for them, and re-layouts  1.67 us (3%)
    pallas_call x1, Pallas kernels, per_device(): pl.pallas_call(functools.partial(block_kernel, n), out_shape=jax.ShapeDty...  64.2 us
    unnamed x1, local copies, waits for them, and re-layouts  1.67 us

profile of v2, /device:TPU:0, one launch (start us, length us, event | category | flops | bytes accessed | tf_op | source)
XLA Modules:
  0.0 65.9 jit_solution(6156749338303852117)
XLA Ops:
  0.0 64.2 %shard_map.73 = bf16[32,4096]{1,0:T(8,128)(2,1)} custom-call(bf16[128,1280]{1,0:T(8,128)(2,1)} %tok_ref.1, s32[4,128]{1,0:T(4,128)} %bitcast.3, bf16[960,1280]{1,0:T(8,128)(2,1)} %bitcast.2, bf16[320,1280]{1,0:T(8,128)(2,1)} %wout_hbm.1, bf16[5120,1024]{1,0:T(8,128)(2,1)} %wmerge_hbm.1, f32[1280]{0:T(1024)} %ga_ref.1, f32[1280]{0:T(1024)} %gm_ref.1), custom_call_target="tpu_custom_call" | custom-call | tf_op jit(solution)/shard_map/pallas_call | solution.py:207
  64.2 1.7 %copy.9 = bf16[32,4096]{1,0:T(8,128)(2,1)} copy(bf16[32,4096]{1,0:T(8,128)(2,1)} %shard_map.73) | data formatting | bytes 524288

commit v3 on v2

--- a/solution.py
+++ b/solution.py
@@ -23,7 +23,7 @@
 def block_kernel(
     n, tok_ref, ids_ref, wqkv_hbm, wout_hbm, wmerge_hbm, ga_ref, gm_ref, out_ref,
     wqkv, wout, wmerge, nslots, qs, ks, vs, key_ids, bias, att, psend, pslots, own, flat, mslots, obuf,
-    local_sem, a_send, a_recv, p_send, p_recv, m_send, m_recv, o_send, o_recv,
+    local_sem, a_send, a_recv, ha_send, ha_recv, p_send, p_recv, m_send, m_recv, o_send, o_recv,
 ):
     me = lax.axis_index("seq")
     dp = lax.axis_index("dp")
@@ -68,6 +68,27 @@
             o_send.at[d], o_recv.at[d], d,
         )
 
+    half_rows = rows // 2
+    half_width = width // 2
+
+    def hop_a(d, half):
+        at = d * rows + half * half_rows
+        source = (1 + half) * rows + half * half_rows if d == 3 else half * half_rows
+        return remote(
+            nslots.at[pl.ds(source, half_rows)], nslots.at[pl.ds(at, half_rows)],
+            ha_send.at[d, half], ha_recv.at[d, half], 2 - half if d == 3 else d,
+        )
+
+    def hop_p(k):
+        return remote(psend.at[k], pslots.at[k], p_send.at[k], p_recv.at[k], (1, 2, 1, 2, 2, 1)[k])
+
+    def hop_m(j, d):
+        source = (1 + j // 2) * quarter if d == 3 else 0
+        return remote(
+            mslots.at[j, pl.ds(source, quarter)], mslots.at[j, pl.ds(d * quarter, quarter)],
+            m_send.at[j, d], m_recv.at[j, d], 2 - j // 2 if d == 3 else d,
+        )
+
     barrier = pltpu.get_barrier_semaphore()
     for d in range(1, n):
         pl.semaphore_signal(barrier, inc=1, device_id=(dp, peer(d)), device_id_type=MESH)
@@ -80,8 +101,13 @@
 
     nslots[0:rows, :] = layer_norm(tok_ref[...].astype(jnp.float32), ga_ref[...].reshape(1, width)).astype(jnp.bfloat16)
     pl.semaphore_wait(barrier, n - 1)
-    for d in range(n - 1, 0, -1):
-        copy_a(d).start()
+    if n == 4:
+        for half in range(2):
+            hop_a(1, half).start()
+            hop_a(2, 1 - half).start()
+    else:
+        for d in range(n - 1, 0, -1):
+            copy_a(d).start()
 
     for d in range(n):
         id_row = ids_ref[pl.ds(peer(d), 1), :].astype(jnp.float32)
@@ -90,7 +116,7 @@
     load_qkv.wait()
     load_out.wait()
 
-    def qkv_step(i, carry):
+    def wait_pair(i):
         for side in range(2):
             d = 2 * i + side
 
@@ -98,6 +124,9 @@
             def _():
                 copy_a(d).wait_recv()
 
+    def qkv_step(i, carry):
+        if n != 4:
+            wait_pair(i)
         at = pl.ds(pl.multiple_of(i * 2 * rows, 2 * rows), 2 * rows)
         for h in range(heads):
             for which in range(3):
@@ -114,12 +143,23 @@
                     vs[h, :, at] = prod.astype(jnp.bfloat16)
         return carry
 
-    lax.fori_loop(0, n // 2, qkv_step, 0)
+    if n == 4:
+        hop_a(1, 0).wait_recv()
+        hop_a(3, 0).start()
+        hop_a(2, 1).wait_recv()
+        hop_a(3, 1).start()
+        hop_a(1, 1).wait_recv()
+        qkv_step(0, 0)
+        hop_a(2, 0).wait_recv()
+        hop_a(3, 0).wait_recv()
+        hop_a(3, 1).wait_recv()
+        qkv_step(1, 0)
+    else:
+        lax.fori_loop(0, n // 2, qkv_step, 0)
 
     factor = HEAD_DIM ** (-0.5) * LOG2E
 
-    def attend_step(i, carry):
-        first = n - 2 - 2 * i
+    def attend(first):
         at = pl.ds(pl.multiple_of(first * rows, 2 * rows), 2 * rows)
         for side in range(2):
             id_row = ids_ref[pl.ds(peer(first + side), 1), :].astype(jnp.float32)
@@ -133,9 +173,13 @@
             row_sum = jnp.sum(expo, axis=0, keepdims=True)
             summed = jnp.dot(vs[h], expo.astype(jnp.bfloat16), preferred_element_type=jnp.float32)
             att[h * HEAD_DIM:(h + 1) * HEAD_DIM, :] = summed / row_sum
-        part = jnp.dot(
+        return jnp.dot(
             att[...].T.astype(jnp.bfloat16), wout[...], preferred_element_type=jnp.float32
         )
+
+    def attend_step(i, carry):
+        first = n - 2 - 2 * i
+        part = attend(first)
         for side in range(1, -1, -1):
             d = first + side
             half = part[side * rows:(side + 1) * rows, :]
@@ -151,29 +195,66 @@
 
         return carry
 
-    lax.fori_loop(0, n // 2, attend_step, 0)
-
-    hidden = own[...] + tok_ref[...].astype(jnp.float32)
-    for d in range(n - 1, 0, -1):
-        copy_p(d).wait_recv()
-        hidden = hidden + pslots[d].astype(jnp.float32)
+    def send_part(k, value):
+        psend[k] = value.astype(jnp.bfloat16)
+        hop_p(k).start()
+
+    tok = tok_ref[...].astype(jnp.float32)
+    if n == 4:
+        part = attend(2)
+        send_part(0, part[rows:, :half_width])
+        send_part(1, part[rows:, half_width:])
+        send_part(3, part[:rows, half_width:])
+        own[:, :half_width] = part[:rows, :half_width]
+        part = attend(0)
+        send_part(2, part[rows:, :half_width])
+        hop_p(1).wait_recv()
+        send_part(5, part[rows:, half_width:] + pslots[1].astype(jnp.float32))
+        hop_p(0).wait_recv()
+        send_part(4, own[:, :half_width] + pslots[0].astype(jnp.float32))
+        own[...] = part[:rows, :] + tok
+        for k in range(2, 6):
+            hop_p(k).wait_recv()
+        left = pslots[2].astype(jnp.float32) + pslots[4].astype(jnp.float32)
+        right = pslots[3].astype(jnp.float32) + pslots[5].astype(jnp.float32)
+        hidden = own[...] + jnp.concatenate([left, right], axis=1)
+    else:
+        lax.fori_loop(0, n // 2, attend_step, 0)
+        hidden = own[...] + tok
+        for d in range(n - 1, 0, -1):
+            copy_p(d).wait_recv()
+            hidden = hidden + pslots[d].astype(jnp.float32)
     normed_two = layer_norm(hidden, gm_ref[...].reshape(1, width))
     lanes = flat.shape[2]
     for c in range(width // lanes):
         flat[c] = normed_two[:, c * lanes:(c + 1) * lanes]
-    for j in range(4):
+    for j in (0, 2, 1, 3):
         for c in range(width // lanes):
             mslots[j, 0:quarter, c * lanes:(c + 1) * lanes] = flat[
                 c, pl.ds(j, quarter, stride=4), :
             ].astype(jnp.bfloat16)
-        for d in range(n - 1, 0, -1):
-            copy_m(j, d).start()
+        if n != 4:
+            for d in range(n - 1, 0, -1):
+                copy_m(j, d).start()
+    if n == 4:
+        for j in range(4):
+            hop_m(j, 1).start()
+            hop_m((j + 2) % 4, 2).start()
+        for j in range(2):
+            hop_m(j, 1).wait_recv()
+            hop_m(j, 3).start()
+            hop_m(j + 2, 2).wait_recv()
+            hop_m(j + 2, 3).start()
 
     load_merge.wait()
     acc = None
-    for j in range(4):
-        for d in range(1, n):
-            copy_m(j, d).wait_recv()
+    for j in (0, 2, 1, 3):
+        if n == 4:
+            hop_m(j, 2 - j // 2).wait_recv()
+            hop_m(j, 3).wait_recv()
+        else:
+            for d in range(1, n):
+                copy_m(j, d).wait_recv()
         part = jnp.dot(
             mslots[j], wmerge[j * width:(j + 1) * width, :], preferred_element_type=jnp.float32
         )
@@ -183,11 +264,20 @@
         copy_o(d).start()
     out_ref[:, pl.ds(pl.multiple_of(me * cols, 128), cols)] = obuf[0:quarter, :]
 
-    for d in range(1, n):
-        copy_a(d).wait_send()
-        copy_p(d).wait_send()
-        for j in range(4):
-            copy_m(j, d).wait_send()
+    if n == 4:
+        for k in range(6):
+            hop_p(k).wait_send()
+        for d in range(1, n):
+            for half in range(2):
+                hop_a(d, half).wait_send()
+            for j in range(4):
+                hop_m(j, d).wait_send()
+    else:
+        for d in range(1, n):
+            copy_a(d).wait_send()
+            copy_p(d).wait_send()
+            for j in range(4):
+                copy_m(j, d).wait_send()
     for d in range(1, n):
         copy_o(d).wait_send()
         copy_o(d).wait_recv()
@@ -200,6 +290,7 @@
     quarter = rows // 4
     cols = w_merge.shape[1]
     total = n * rows
+    exchange = (6, rows, width // 2) if n == 4 else (n, rows, width)
     vmem = pl.BlockSpec(memory_space=pltpu.VMEM)
     hbm = pl.BlockSpec(memory_space=pl.ANY)
     bf16 = jnp.bfloat16
@@ -220,8 +311,8 @@
             pltpu.VMEM((total, rows), jnp.float32),
             pltpu.VMEM((total, 2 * rows), jnp.float32),
             pltpu.VMEM((heads * HEAD_DIM, 2 * rows), jnp.float32),
-            pltpu.VMEM((n, rows, width), bf16),
-            pltpu.VMEM((n, rows, width), bf16),
+            pltpu.VMEM(exchange, bf16),
+            pltpu.VMEM(exchange, bf16),
             pltpu.VMEM((rows, width), jnp.float32),
             pltpu.VMEM((width // 128, rows, 128), jnp.float32),
             pltpu.VMEM((4, n * quarter, width), bf16),
@@ -229,8 +320,10 @@
             dma((3,)),
             dma((n,)),
             dma((n,)),
-            dma((n,)),
-            dma((n,)),
+            dma((n, 2)),
+            dma((n, 2)),
+            dma(exchange[:1]),
+            dma(exchange[:1]),
             dma((4, n)),
             dma((4, n)),
             dma((n,)),

time: 66.1 us -> 52.2 us (0.79)
  Pallas kernels: 64.2 us -> 50.4 us
    pallas_call x1, Pallas kernels: 64.2 us -> 50.4 us  [per_device(): pl.pallas_call(functools.partial(block_kernel, n), out_shape=jax.ShapeDty...]
where the time goes in v3:
time: 52.2 us; the launch traced here: 52 us
  Pallas kernels  50.4 us (97%)
  local copies, waits for them, and re-layouts  1.67 us (3%)
    pallas_call x1, Pallas kernels, per_device(): pl.pallas_call(functools.partial(block_kernel, n), out_shape=jax.ShapeDty...  50.4 us
    unnamed x1, local copies, waits for them, and re-layouts  1.67 us

profile of v3, /device:TPU:0, one launch (start us, length us, event | category | flops | bytes accessed | tf_op | source)
XLA Modules:
  0.0 52.0 jit_solution(11543287969390194695)
XLA Ops:
  0.0 50.4 %shard_map.73 = bf16[32,4096]{1,0:T(8,128)(2,1)} custom-call(bf16[128,1280]{1,0:T(8,128)(2,1)} %tok_ref.1, s32[4,128]{1,0:T(4,128)} %bitcast.3, bf16[960,1280]{1,0:T(8,128)(2,1)} %bitcast.2, bf16[320,1280]{1,0:T(8,128)(2,1)} %wout_hbm.1, bf16[5120,1024]{1,0:T(8,128)(2,1)} %wmerge_hbm.1, f32[1280]{0:T(1024)} %ga_ref.1, f32[1280]{0:T(1024)} %gm_ref.1), custom_call_target="tpu_custom_call" | custom-call | tf_op jit(solution)/shard_map/pallas_call | solution.py:298
  50.4 1.7 %copy.9 = bf16[32,4096]{1,0:T(8,128)(2,1)} copy(bf16[32,4096]{1,0:T(8,128)(2,1)} %shard_map.73) | data formatting | bytes 524288

commit v4 on v3

--- a/solution.py
+++ b/solution.py
@@ -52,7 +52,7 @@
         )
 
     def copy_p(d):
-        return remote(psend.at[d], pslots.at[d], p_send.at[d], p_recv.at[d], d)
+        return remote(psend.at[d], pslots.at[d], p_send.at[d, 0], p_recv.at[d, 0], d)
 
     def copy_m(j, d):
         return remote(
@@ -65,7 +65,7 @@
         return remote(
             obuf.at[pl.ds(d * quarter, quarter)],
             out_ref.at[:, pl.ds(pl.multiple_of(me * cols, 128), cols)],
-            o_send.at[d], o_recv.at[d], d,
+            o_send.at[0, d], o_recv.at[0, d], d,
         )
 
     half_rows = rows // 2
@@ -79,14 +79,29 @@
             ha_send.at[d, half], ha_recv.at[d, half], 2 - half if d == 3 else d,
         )
 
-    def hop_p(k):
-        return remote(psend.at[k], pslots.at[k], p_send.at[k], p_recv.at[k], (1, 2, 1, 2, 2, 1)[k])
-
-    def hop_m(j, d):
-        source = (1 + j // 2) * quarter if d == 3 else 0
-        return remote(
-            mslots.at[j, pl.ds(source, quarter)], mslots.at[j, pl.ds(d * quarter, quarter)],
-            m_send.at[j, d], m_recv.at[j, d], 2 - j // 2 if d == 3 else d,
+    def hop_p(k, r):
+        at = pl.ds(r * half_rows, half_rows)
+        return remote(
+            psend.at[k, at], pslots.at[k, at], p_send.at[k, r], p_recv.at[k, r],
+            (1, 2, 1, 2, 2, 1)[k],
+        )
+
+    eighth = quarter // 2
+
+    def hop_m(r, g, d):
+        source = (1 + g) * quarter + r * eighth if d == 3 else r * eighth
+        pair = pl.ds(2 * g, 2)
+        return remote(
+            mslots.at[pair, pl.ds(source, eighth)],
+            mslots.at[pair, pl.ds(d * quarter + r * eighth, eighth)],
+            m_send.at[2 * r + g, d], m_recv.at[2 * r + g, d], 2 - g if d == 3 else d,
+        )
+
+    def hop_o(r, d):
+        return remote(
+            obuf.at[pl.ds((r * n + d) * eighth, eighth)],
+            out_ref.at[pl.ds(r * eighth, eighth), pl.ds(pl.multiple_of(me * cols, 128), cols)],
+            o_send.at[r, d], o_recv.at[r, d], d,
         )
 
     barrier = pltpu.get_barrier_semaphore()
@@ -195,92 +210,128 @@
 
         return carry
 
-    def send_part(k, value):
-        psend[k] = value.astype(jnp.bfloat16)
-        hop_p(k).start()
+    def send_part(k, r, value):
+        psend[k, r * half_rows:(r + 1) * half_rows, :] = value.astype(jnp.bfloat16)
+        hop_p(k, r).start()
+
+    def came(k, r):
+        return pslots[k, r * half_rows:(r + 1) * half_rows, :].astype(jnp.float32)
+
+    lanes = flat.shape[2]
+
+    def put_merged(first, count, value):
+        for c in range(width // lanes):
+            flat[c, first:first + count, :] = value[:, c * lanes:(c + 1) * lanes]
+        for j in range(4):
+            for c in range(width // lanes):
+                mslots[j, first // 4:(first + count) // 4, c * lanes:(c + 1) * lanes] = flat[
+                    c, pl.ds(first + j, count // 4, stride=4), :
+                ].astype(jnp.bfloat16)
 
     tok = tok_ref[...].astype(jnp.float32)
+    mine = pl.ds(pl.multiple_of(me * cols, 128), cols)
     if n == 4:
+        halves = [(r, slice(r * half_rows, (r + 1) * half_rows)) for r in range(2)]
         part = attend(2)
-        send_part(0, part[rows:, :half_width])
-        send_part(1, part[rows:, half_width:])
-        send_part(3, part[:rows, half_width:])
-        own[:, :half_width] = part[:rows, :half_width]
+        near, far = part[:rows, :], part[rows:, :]
+        for r, at in halves:
+            send_part(0, r, far[at, :half_width])
+            send_part(1, r, far[at, half_width:])
+        for r, at in halves:
+            send_part(3, r, near[at, half_width:])
+        own[:, :half_width] = near[:, :half_width]
         part = attend(0)
-        send_part(2, part[rows:, :half_width])
-        hop_p(1).wait_recv()
-        send_part(5, part[rows:, half_width:] + pslots[1].astype(jnp.float32))
-        hop_p(0).wait_recv()
-        send_part(4, own[:, :half_width] + pslots[0].astype(jnp.float32))
-        own[...] = part[:rows, :] + tok
-        for k in range(2, 6):
-            hop_p(k).wait_recv()
-        left = pslots[2].astype(jnp.float32) + pslots[4].astype(jnp.float32)
-        right = pslots[3].astype(jnp.float32) + pslots[5].astype(jnp.float32)
-        hidden = own[...] + jnp.concatenate([left, right], axis=1)
+        near, far = part[:rows, :], part[rows:, :]
+        for r, at in halves:
+            send_part(2, r, far[at, :half_width])
+            hop_p(1, r).wait_recv()
+            send_part(5, r, far[at, half_width:] + came(1, r))
+            hop_p(0, r).wait_recv()
+            send_part(4, r, own[at, :half_width] + came(0, r))
+        own[...] = near + tok
+        for r, at in halves:
+            for k in range(2, 6):
+                hop_p(k, r).wait_recv()
+            summed = jnp.concatenate(
+                [came(2, r) + came(4, r), came(3, r) + came(5, r)], axis=1
+            )
+            hidden = own[at, :] + summed
+            put_merged(
+                r * half_rows, half_rows, layer_norm(hidden, gm_ref[...].reshape(1, width))
+            )
+            for g in range(2):
+                hop_m(r, g, 1).start()
+                hop_m(r, 1 - g, 2).start()
+        for r in range(2):
+            hop_m(r, 0, 1).wait_recv()
+            hop_m(r, 0, 3).start()
+            hop_m(r, 1, 2).wait_recv()
+            hop_m(r, 1, 3).start()
+        load_merge.wait()
+        for r in range(2):
+            acc = None
+            for j in range(4):
+                if j % 2 == 0:
+                    hop_m(r, j // 2, 2 - j // 2).wait_recv()
+                    hop_m(r, j // 2, 3).wait_recv()
+                block = jnp.concatenate(
+                    [
+                        mslots[j, d * quarter + r * eighth:d * quarter + (r + 1) * eighth, :]
+                        for d in range(n)
+                    ],
+                    axis=0,
+                )
+                part = jnp.dot(
+                    block, wmerge[j * width:(j + 1) * width, :],
+                    preferred_element_type=jnp.float32,
+                )
+                acc = part if acc is None else acc + part
+            obuf[r * n * eighth:(r + 1) * n * eighth, :] = acc.astype(jnp.bfloat16)
+            for d in range(n - 1, 0, -1):
+                hop_o(r, d).start()
+            out_ref[r * eighth:(r + 1) * eighth, mine] = obuf[
+                r * n * eighth:r * n * eighth + eighth, :
+            ]
+        for r in range(2):
+            for k in range(6):
+                hop_p(k, r).wait_send()
+            for d in range(1, n):
+                hop_a(d, r).wait_send()
+                for g in range(2):
+                    hop_m(r, g, d).wait_send()
+                hop_o(r, d).wait_send()
+                hop_o(r, d).wait_recv()
     else:
         lax.fori_loop(0, n // 2, attend_step, 0)
         hidden = own[...] + tok
         for d in range(n - 1, 0, -1):
             copy_p(d).wait_recv()
             hidden = hidden + pslots[d].astype(jnp.float32)
-    normed_two = layer_norm(hidden, gm_ref[...].reshape(1, width))
-    lanes = flat.shape[2]
-    for c in range(width // lanes):
-        flat[c] = normed_two[:, c * lanes:(c + 1) * lanes]
-    for j in (0, 2, 1, 3):
-        for c in range(width // lanes):
-            mslots[j, 0:quarter, c * lanes:(c + 1) * lanes] = flat[
-                c, pl.ds(j, quarter, stride=4), :
-            ].astype(jnp.bfloat16)
-        if n != 4:
+        put_merged(0, rows, layer_norm(hidden, gm_ref[...].reshape(1, width)))
+        for j in range(4):
             for d in range(n - 1, 0, -1):
                 copy_m(j, d).start()
-    if n == 4:
+        load_merge.wait()
+        acc = None
         for j in range(4):
-            hop_m(j, 1).start()
-            hop_m((j + 2) % 4, 2).start()
-        for j in range(2):
-            hop_m(j, 1).wait_recv()
-            hop_m(j, 3).start()
-            hop_m(j + 2, 2).wait_recv()
-            hop_m(j + 2, 3).start()
-
-    load_merge.wait()
-    acc = None
-    for j in (0, 2, 1, 3):
-        if n == 4:
-            hop_m(j, 2 - j // 2).wait_recv()
-            hop_m(j, 3).wait_recv()
-        else:
             for d in range(1, n):
                 copy_m(j, d).wait_recv()
-        part = jnp.dot(
-            mslots[j], wmerge[j * width:(j + 1) * width, :], preferred_element_type=jnp.float32
-        )
-        acc = part if acc is None else acc + part
-    obuf[...] = acc.astype(jnp.bfloat16)
-    for d in range(n - 1, 0, -1):
-        copy_o(d).start()
-    out_ref[:, pl.ds(pl.multiple_of(me * cols, 128), cols)] = obuf[0:quarter, :]
-
-    if n == 4:
-        for k in range(6):
-            hop_p(k).wait_send()
-        for d in range(1, n):
-            for half in range(2):
-                hop_a(d, half).wait_send()
-            for j in range(4):
-                hop_m(j, d).wait_send()
-    else:
+            part = jnp.dot(
+                mslots[j], wmerge[j * width:(j + 1) * width, :],
+                preferred_element_type=jnp.float32,
+            )
+            acc = part if acc is None else acc + part
+        obuf[...] = acc.astype(jnp.bfloat16)
+        for d in range(n - 1, 0, -1):
+            copy_o(d).start()
+        out_ref[:, mine] = obuf[0:quarter, :]
         for d in range(1, n):
             copy_a(d).wait_send()
             copy_p(d).wait_send()
             for j in range(4):
                 copy_m(j, d).wait_send()
-    for d in range(1, n):
-        copy_o(d).wait_send()
-        copy_o(d).wait_recv()
+            copy_o(d).wait_send()
+            copy_o(d).wait_recv()
 
 
 def per_device(tokens, segment_ids, w_qkv, w_out, w_merge, gain_attn, gain_merge):
@@ -322,12 +373,12 @@
             dma((n,)),
             dma((n, 2)),
             dma((n, 2)),
-            dma(exchange[:1]),
-            dma(exchange[:1]),
+            dma((exchange[0], 2)),
+            dma((exchange[0], 2)),
             dma((4, n)),
             dma((4, n)),
-            dma((n,)),
-            dma((n,)),
+            dma((2, n)),
+            dma((2, n)),
         ],
         compiler_params=pltpu.CompilerParams(
             collective_id=0, has_side_effects=True, vmem_limit_bytes=56 * 1024 * 1024

time: 52.2 us -> 53.4 us (1.023)
  Pallas kernels: 50.4 us -> 51.6 us
    pallas_call x1, Pallas kernels: 50.4 us -> 51.6 us  [per_device(): pl.pallas_call(functools.partial(block_kernel, n), out_shape=jax.ShapeDty...]
where the time goes in v4:
time: 53.4 us; the launch traced here: 53.2 us
  Pallas kernels  51.6 us (97%)
  local copies, waits for them, and re-layouts  1.67 us (3%)
    pallas_call x1, Pallas kernels, per_device(): pl.pallas_call(functools.partial(block_kernel, n), out_shape=jax.ShapeDty...  51.6 us
    unnamed x1, local copies, waits for them, and re-layouts  1.67 us

profile of v4, /device:TPU:0, one launch (start us, length us, event | category | flops | bytes accessed | tf_op | source)
XLA Modules:
  0.0 53.2 jit_solution(1408954045597072435)
XLA Ops:
  0.0 51.6 %shard_map.73 = bf16[32,4096]{1,0:T(8,128)(2,1)} custom-call(bf16[128,1280]{1,0:T(8,128)(2,1)} %tok_ref.1, s32[4,128]{1,0:T(4,128)} %bitcast.3, bf16[960,1280]{1,0:T(8,128)(2,1)} %bitcast.2, bf16[320,1280]{1,0:T(8,128)(2,1)} %wout_hbm.1, bf16[5120,1024]{1,0:T(8,128)(2,1)} %wmerge_hbm.1, f32[1280]{0:T(1024)} %ga_ref.1, f32[1280]{0:T(1024)} %gm_ref.1), custom_call_target="tpu_custom_call" | custom-call | tf_op jit(solution)/shard_map/pallas_call | solution.py:349
  51.6 1.7 %copy.9 = bf16[32,4096]{1,0:T(8,128)(2,1)} copy(bf16[32,4096]{1,0:T(8,128)(2,1)} %shard_map.73) | data formatting | bytes 524288

commit v5 on v3

--- a/solution.py
+++ b/solution.py
@@ -128,19 +128,18 @@
         if n != 4:
             wait_pair(i)
         at = pl.ds(pl.multiple_of(i * 2 * rows, 2 * rows), 2 * rows)
+        prod = lax.dot_general(
+            wqkv[...], nslots[at, :], (((1,), (1,)), ((), ())),
+            preferred_element_type=jnp.float32,
+        )
         for h in range(heads):
-            for which in range(3):
-                base = HEAD_DIM * (3 * h + which)
-                prod = lax.dot_general(
-                    wqkv[base:base + HEAD_DIM, :], nslots[at, :], (((1,), (1,)), ((), ())),
-                    preferred_element_type=jnp.float32,
-                )
-                if which == 0:
-                    qs[h, :, at] = prod.astype(jnp.bfloat16)
-                elif which == 1:
-                    ks[h, at, :] = prod.T.astype(jnp.bfloat16)
-                else:
-                    vs[h, :, at] = prod.astype(jnp.bfloat16)
+            base = 3 * HEAD_DIM * h
+            query = prod[base:base + HEAD_DIM, :]
+            key = prod[base + HEAD_DIM:base + 2 * HEAD_DIM, :]
+            value = prod[base + 2 * HEAD_DIM:base + 3 * HEAD_DIM, :]
+            qs[h, :, at] = query.astype(jnp.bfloat16)
+            ks[h, at, :] = key.T.astype(jnp.bfloat16)
+            vs[h, :, at] = value.astype(jnp.bfloat16)
         return carry
 
     if n == 4:

time: 52.2 us -> 51.1 us (0.979)
  Pallas kernels: 50.4 us -> 49.2 us
    pallas_call x1, Pallas kernels: 50.4 us -> 49.2 us  [per_device(): pl.pallas_call(functools.partial(block_kernel, n), out_shape=jax.ShapeDty...]
where the time goes in v5:
time: 51.1 us; the launch traced here: 50.9 us
  Pallas kernels  49.2 us (96%)
  local copies, waits for them, and re-layouts  1.67 us (3%)
    pallas_call x1, Pallas kernels, per_device(): pl.pallas_call(functools.partial(block_kernel, n), out_shape=jax.ShapeDty...  49.2 us
    unnamed x1, local copies, waits for them, and re-layouts  1.67 us

profile of v5, /device:TPU:0, one launch (start us, length us, event | category | flops | bytes accessed | tf_op | source)
XLA Modules:
  0.0 50.9 jit_solution(16058147636967687014)
XLA Ops:
  0.0 49.2 %shard_map.73 = bf16[32,4096]{1,0:T(8,128)(2,1)} custom-call(bf16[128,1280]{1,0:T(8,128)(2,1)} %tok_ref.1, s32[4,128]{1,0:T(4,128)} %bitcast.3, bf16[960,1280]{1,0:T(8,128)(2,1)} %bitcast.2, bf16[320,1280]{1,0:T(8,128)(2,1)} %wout_hbm.1, bf16[5120,1024]{1,0:T(8,128)(2,1)} %wmerge_hbm.1, f32[1280]{0:T(1024)} %ga_ref.1, f32[1280]{0:T(1024)} %gm_ref.1), custom_call_target="tpu_custom_call" | custom-call | tf_op jit(solution)/shard_map/pallas_call | solution.py:297
  49.2 1.7 %copy.9 = bf16[32,4096]{1,0:T(8,128)(2,1)} copy(bf16[32,4096]{1,0:T(8,128)(2,1)} %shard_map.73) | data formatting | bytes 524288
